TPU v7x, 128 devices: a whole 4x4x4 slice. The times are simulated.
128 devices in a mesh: dp: 32 (over z, x, core), mp: 4 (over y).
Axes of the slice: x: 4, y: 4, z: 4, core: 2. Of those that a mesh axis runs over, the one named last changes fastest.
Arguments:
- candidates: int32 [512, 3], P('dp'), may hold values from 0 to 31, as said below
- row_lengths: int32 [512, 2], P('dp'), may hold values from 1 to 128
- enc_bank: bfloat16 [512, 128, 2048], P('dp', None, 'mp'), may hold values from -480 to 480
- dec_bank: bfloat16 [512, 128, 2048], P('dp', None, 'mp'), may hold values from -6 to 6
- w_query: bfloat16 [2048, 2048], P(None, 'mp'), may hold values from -0.125 to 0.125
- w_key: bfloat16 [2048, 2048], P(None, 'mp'), may hold values from -0.125 to 0.125
- w_value: bfloat16 [2048, 2048], P(None, 'mp'), may hold values from -0.125 to 0.125
Outputs:
- contexts: bfloat16 [768, 128, 2048], P('dp', None, 'mp')
Inputs may be any that keep to these rules, and one draw needn't show every extreme that they name: `candidates`: row ids in columns 0 and 1 index the same shard's banks (0 to 15), column 2 is a group (0 to 31). A shard sends either none or exactly 2 pairs to a group; a group receives at most 24 pairs in all, and some group exactly 24.
All inputs are finite; a program needn't handle non-finite values.
Results may differ from a plain program's by a relative error of at most 0.0045.
The roundings to bfloat16 on the way count: a program that leaves them out, or rounds other values in their place, can miss the bound.
Values may be sent and summed in bfloat16 or wider, within the bound.
No kernel may reach another device: no remote copies, remote signals or barrier semaphores. Data moves between devices by JAX's collectives and lax.ppermute only.
A program may use at most 128 MiB of HBM per device.

v0:
```python
import math
import jax
import jax.numpy as jnp
from jax import lax
from jax.sharding import PartitionSpec as P

D = 2048
HD = 128
L = 128
CAP = 2


def attend(source_rows, target_rows, source_length, target_length, w_query, w_key, w_value):
    pair_count = target_rows.shape[0]
    local_width = w_query.shape[1]
    head_count = local_width // HD
    rows_f = target_rows.astype(jnp.float32)
    row_mean = jnp.mean(rows_f, axis=-1, keepdims=True)
    centred = rows_f - row_mean
    variance = jnp.mean(centred * centred, axis=-1, keepdims=True)
    normed = (centred * lax.rsqrt(variance + 1e-05)).astype(jnp.bfloat16)
    queries = jnp.dot(normed.reshape(-1, D), w_query, preferred_element_type=jnp.float32).astype(
        jnp.bfloat16
    )
    key_rows = jnp.dot(
        source_rows.reshape(-1, D), w_key, preferred_element_type=jnp.float32
    ).astype(jnp.bfloat16)
    value_rows = jnp.dot(
        source_rows.reshape(-1, D), w_value, preferred_element_type=jnp.float32
    ).astype(jnp.bfloat16)
    queries = queries.reshape(pair_count, L, head_count, HD)
    key_rows = key_rows.reshape(pair_count, L, head_count, HD)
    value_rows = value_rows.reshape(pair_count, L, head_count, HD)
    scores = jnp.einsum(
        "plhd,pmhd->phlm", queries, key_rows, preferred_element_type=jnp.float32
    ) * (1.0 / math.sqrt(HD))
    positions = jnp.arange(L, dtype=jnp.int32)
    key_mask = positions[None, None, None, :] < source_length[:, None, None, None]
    scores = jnp.where(key_mask, scores, -1e30)
    biggest = jnp.max(scores, axis=-1, keepdims=True)
    expo_terms = jnp.exp(scores - biggest)
    totals = jnp.sum(expo_terms, axis=-1, keepdims=True)
    attn_weights = (expo_terms / totals).astype(jnp.bfloat16)
    context = jnp.einsum(
        "phlm,pmhd->plhd", attn_weights, value_rows, preferred_element_type=jnp.float32
    )
    query_mask = positions[None, :, None, None] < target_length[:, None, None, None]
    context = jnp.where(query_mask, context, 0.0).astype(jnp.bfloat16)
    return context.reshape(pair_count, L, local_width)


def compact(flags, capacity):
    flags_flat = flags.reshape(-1).astype(jnp.int32)
    before = jnp.cumsum(flags_flat) - flags_flat
    wanted = jnp.arange(capacity, dtype=jnp.int32)
    hit_table = (before[None, :] == wanted[:, None]) & (flags_flat[None, :] == 1)
    received_ids = jnp.arange(flags_flat.shape[0], dtype=jnp.int32)
    source = jnp.sum(jnp.where(hit_table, received_ids[None, :], 0), axis=1)
    usable = jnp.any(hit_table, axis=1)
    return (source, usable)


def on_device(candidates, row_lengths, enc_bank, dec_bank, w_query, w_key, w_value):
    shards = lax.axis_size("dp")
    cand_count = candidates.shape[0]
    local_width = enc_bank.shape[2]
    groups_each = cand_count // CAP
    hot_groups = min(3 * groups_each // 4, shards // 2)
    capacity = 2 * CAP * max(hot_groups, groups_each - hot_groups)
    source_ids = candidates[:, 0]
    target_ids = candidates[:, 1]
    destination = candidates[:, 2]
    cand_ids = jnp.arange(cand_count, dtype=jnp.int32)
    same_dest = destination[:, None] == destination[None, :]
    rank_in = jnp.sum(same_dest & (cand_ids[None, :] < cand_ids[:, None]), axis=1)
    group_ids = jnp.arange(shards, dtype=jnp.int32)
    slot_ids = jnp.arange(CAP, dtype=jnp.int32)
    matches = (destination[None, None, :] == group_ids[:, None, None]) & (
        rank_in[None, None, :] == slot_ids[None, :, None]
    )
    filled = jnp.any(matches, axis=-1)
    picked = jnp.sum(jnp.where(matches, cand_ids[None, None, :], 0), axis=-1)
    source_length = jnp.take(row_lengths[:, 0], source_ids, axis=0)
    target_length = jnp.take(row_lengths[:, 1], target_ids, axis=0)
    send_source = jnp.take(enc_bank, jnp.take(source_ids, picked, axis=0), axis=0)
    send_target = jnp.take(dec_bank, jnp.take(target_ids, picked, axis=0), axis=0)
    pair_lengths = jnp.stack(
        [jnp.take(source_length, picked, axis=0), jnp.take(target_length, picked, axis=0)], axis=-1
    )
    send_lengths = jnp.where(filled[:, :, None], pair_lengths, 0).astype(jnp.bfloat16)
    got_source, got_target, got_lengths = (
        lax.all_to_all(send_source, "dp", split_axis=0, concat_axis=0, tiled=True),
        lax.all_to_all(send_target, "dp", split_axis=0, concat_axis=0, tiled=True),
        lax.all_to_all(send_lengths, "dp", split_axis=0, concat_axis=0, tiled=True),
    )
    source, usable = compact(got_lengths[:, :, 1] > 0.5, capacity)
    rows_source = jnp.take(got_source.reshape(-1, L, local_width), source, axis=0)
    rows_target = jnp.take(got_target.reshape(-1, L, local_width), source, axis=0)
    lengths_got = jnp.take(got_lengths.reshape(-1, 2), source, axis=0).astype(jnp.int32)
    lengths_got = jnp.where(usable[:, None], lengths_got, 0)
    full_source, full_target = (
        lax.all_gather(rows_source, "mp", axis=2, tiled=True),
        lax.all_gather(rows_target, "mp", axis=2, tiled=True),
    )
    result = attend(
        full_source,
        full_target,
        jnp.maximum(lengths_got[:, 0], 1),
        lengths_got[:, 1],
        w_query,
        w_key,
        w_value,
    )
    return result


def solution(mesh):
    placed = (
        P("dp", None),
        P("dp", None),
        P("dp", None, "mp"),
        P("dp", None, "mp"),
        P(None, "mp"),
        P(None, "mp"),
        P(None, "mp"),
    )
    return jax.shard_map(
        on_device, mesh=mesh, in_specs=placed, out_specs=P("dp", None, "mp"), check_vma=False
    )
```

profile of v0, /device:TPU:1, one launch (start us, length us, event | category | flops | bytes accessed | tf_op | source)
XLA Modules:
  0.0 571.5 jit_solution(15332898626109545930)
XLA Ops:
  6.5 0.9 slice_bitcast_fusion.2
  7.5 0.2 convert_reduce_fusion.1
  7.7 0.8 compare_select_fusion.4
  8.4 0.1 fusion.17
  8.5 0.1 and_reduce_fusion
  8.6 0.1 copy.43
  8.7 0.1 reshape.363
  8.9 0.8 gather_fusion.8
  9.6 0.1 reshape.386
  9.7 0.1 copy.56
  9.9 0.7 gather_fusion.1
  10.5 0.7 gather_fusion.3
  11.2 0.8 gather_fusion.2
  12.0 0.1 reshape.366
  12.1 0.1 copy.44
  12.2 0.8 gather_fusion.4
  13.0 0.1 reshape.372
  13.1 0.1 copy.46
  13.2 0.7 copy.47
  13.9 9.4 %all-to-all-start = ((bf16[32,2,2]{1,2,0:T(2,128)(2,1)}), bf16[32,2,2]{1,2,0:T(2,128)(2,1)S(1)}, u32[]{:S(2)}, u32[]{:S(2)}) async-start(bf16[32,2,2]{1,2,0:T(2,128)(2,1)} %copy.47), calls=%async_computation | async-start | bytes 32768 | tf_op jit(solution)/shard_map/all_to_all | solution.py:94
  23.4 0.8 gather_fusion.5
  24.1 0.1 reshape.376
  24.3 0.1 copy.54
  24.4 0.1 reshape.377
  24.5 0.1 copy.53
  24.7 5.3 gather_fusion.6
  30.0 7.5 %broadcast_select_fusion.1 = bf16[32,2,128,512]{3,2,1,0:T(8,128)(2,1)} fusion(bf16[32,2,128,512]{3,2,1,0:T(8,128)(2,1)} %bitcast.43, pred[32,2]{1,0:T(8,128)(4,1)S(1)} %copy.53), kind=kLoop, calls=%fused_computation.19 | loop fusion | flops 4194304 | bytes 16777280 | tf_op jit(solution)/shard_map/jit(_take)/select_n | solution.py:85
  37.5 7.6 %all-to-all-start.1 = ((bf16[32,2,128,512]{3,2,1,0:T(8,128)(2,1)}), bf16[32,2,128,512]{3,2,1,0:T(8,128)(2,1)}, u32[]{:S(2)}, u32[]{:S(2)}) async-start(bf16[32,2,128,512]{3,2,1,0:T(8,128)(2,1)} %broadcast_select_fusion.1), calls=%async_computation.1 | async-start | bytes 16777216 | tf_op jit(solution)/shard_map/all_to_all | solution.py:92
  45.1 0.1 copy.58
  45.1 0.1 reshape.387
  45.2 0.1 copy.57
  45.4 5.3 gather_fusion.9
  50.7 7.5 %broadcast_select_fusion = bf16[32,2,128,512]{3,2,1,0:T(8,128)(2,1)} fusion(bf16[32,2,128,512]{3,2,1,0:T(8,128)(2,1)} %bitcast.44, pred[32,2]{1,0:T(8,128)(4,1)S(1)} %copy.57), kind=kLoop, calls=%fused_computation.18 | loop fusion | flops 4194304 | bytes 16777280 | tf_op jit(solution)/shard_map/jit(_take)/select_n | solution.py:86
  58.2 86.6 %all-to-all-done.1 = bf16[32,2,128,512]{3,2,1,0:T(8,128)(2,1)} async-done(((bf16[32,2,128,512]{3,2,1,0:T(8,128)(2,1)}), bf16[32,2,128,512]{3,2,1,0:T(8,128)(2,1)}, u32[]{:S(2)}, u32[]{:S(2)}) %all-to-all-start.1) | async-done | bytes 8388640 | tf_op jit(solution)/shard_map/all_to_all | solution.py:92
  144.8 11.0 %all-to-all-start.2 = ((bf16[32,2,128,512]{3,2,1,0:T(8,128)(2,1)}), bf16[32,2,128,512]{3,2,1,0:T(8,128)(2,1)}, u32[]{:S(2)}, u32[]{:S(2)}) async-start(bf16[32,2,128,512]{3,2,1,0:T(8,128)(2,1)} %broadcast_select_fusion), calls=%async_computation.2 | async-start | bytes 16777216 | tf_op jit(solution)/shard_map/all_to_all | solution.py:93
  156.0 0.1 reduce-window.8
  156.1 0.1 reduce.1
  156.2 0.1 reshape.256
  156.4 0.1 select_reduce_fusion
  156.5 6.0 %gather_fusion.7 = bf16[24,128,512]{2,1,0:T(8,128)(2,1)} fusion(bf16[64,128,512]{2,1,0:T(8,128)(2,1)} %bitcast.11, s32[1024]{0:T(1024)S(1)} %pad_clamp_fusion.1), kind=kCustom, calls=%fused_computation.3.clone | custom fusion | bytes 6291552 | tf_op jit(solution)/shard_map/jit(_take)/gather | solution.py:97
  162.5 93.1 %all-to-all-done.2 = bf16[32,2,128,512]{3,2,1,0:T(8,128)(2,1)} async-done(((bf16[32,2,128,512]{3,2,1,0:T(8,128)(2,1)}), bf16[32,2,128,512]{3,2,1,0:T(8,128)(2,1)}, u32[]{:S(2)}, u32[]{:S(2)}) %all-to-all-start.2) | async-done | bytes 8388640 | tf_op jit(solution)/shard_map/all_to_all | solution.py:93
  255.6 5.9 %gather_fusion.10 = bf16[24,128,512]{2,1,0:T(8,128)(2,1)} fusion(bf16[64,128,512]{2,1,0:T(8,128)(2,1)} %bitcast.14, s32[1024]{0:T(1024)S(1)} %pad_clamp_fusion.1), kind=kCustom, calls=%fused_computation.9.clone | custom fusion | bytes 6291552 | tf_op jit(solution)/shard_map/jit(_take)/gather | solution.py:98
  261.5 6.3 %broadcast_select_fusion.2 = (bf16[24,128,512]{2,1,0:T(8,128)(2,1)}, bf16[24,128,512]{2,1,0:T(8,128)(2,1)}) fusion(bf16[24,128,512]{2,1,0:T(8,128)(2,1)} %gather_fusion.10, pred[24]{0:T(512)(128)(4,1)S(1)} %compare_and_fusion.3, bf16[24,128,512]{2,1,0:T(8,128)(2,1)} %gather_fusion.7), kind=kLoop, calls=%fused_computation.36 | loop fusion | flops 3145728 | bytes 12582936 | tf_op jit(solution)/shard_map/jit(_take)/select_n | solution.py:98
  267.7 0.2 all-gather.3.cloned.1.call-start
  268.0 0.5 all-gather.3.cloned.1.call-update
  268.5 0.3 copy.65
  268.8 0.6 gather_fusion
  269.4 0.1 fusion.20
  269.6 0.2 fusion.18
  269.9 119.2 %all-gather.5.cloned.1.call-done = bf16[24,128,2048]{2,1,0:T(8,128)(2,1)} async-done(((bf16[24,128,512]{2,1,0:T(8,128)(2,1)}), bf16[24,128,2048]{2,1,0:T(8,128)(2,1)}) %all-gather.5.cloned.1.call-update) | async-done | bytes 12582928 | tf_op jit(solution)/shard_map/all_gather | solution.py:103
  389.1 6.3 %convert_reduce_fusion = f32[24,128]{1,0:T(8,128)S(1)} fusion(bf16[24,128,2048]{2,1,0:T(8,128)(2,1)} %all-gather.5.cloned.1.call-done), kind=kLoop, calls=%fused_computation.13 | loop fusion | flops 12579840 | bytes 12595200 | tf_op jit(solution)/shard_map/reduce_sum | solution.py:18
  395.4 8.0 %fusion.3 = f32[24,128]{1,0:T(8,128)S(1)} fusion(bf16[24,128,2048]{2,1,0:T(8,128)(2,1)} %all-gather.5.cloned.1.call-done, f32[24,128]{1,0:T(8,128)S(1)} %broadcast_multiply_fusion), kind=kLoop, calls=%fused_computation.16 | loop fusion | flops 25162752 | bytes 12607488 | tf_op jit(solution)/shard_map/reduce_sum | solution.py:20
  403.4 8.9 %fusion.4 = bf16[24,128,2048]{2,1,0:T(8,128)(2,1)S(1)} fusion(bf16[24,128,2048]{2,1,0:T(8,128)(2,1)} %all-gather.5.cloned.1.call-done, f32[24,128]{1,0:T(8,128)S(1)} %add_rsqrt_fusion, f32[24,128]{1,0:T(8,128)S(1)} %broadcast_multiply_fusion), kind=kLoop, calls=%fused_computation.17 | loop fusion | flops 25165824 | bytes 25190400 | tf_op jit(solution)/shard_map/convert_element_type | solution.py:21
  412.4 8.1 %convolution_convert_fusion.1 = bf16[3072,512]{1,0:T(8,128)(2,1)} fusion(bf16[3072,2048]{1,0:T(8,128)(2,1)S(1)} %bitcast.45, bf16[2048,512]{1,0:T(8,128)(2,1)S(1)} %copy-done.6), kind=kOutput, calls=%fused_computation.26 | convolution fusion | flops 6444023808 | bytes 17825792 | tf_op jit(solution)/shard_map/dot_general | solution.py:22
  420.5 5.5 reshape.252
  426.0 84.3 %all-gather.3.cloned.1.call-done = bf16[24,128,2048]{2,1,0:T(8,128)(2,1)} async-done(((bf16[24,128,512]{2,1,0:T(8,128)(2,1)}), bf16[24,128,2048]{2,1,0:T(8,128)(2,1)}) %all-gather.3.cloned.1.call-update) | async-done | bytes 12582928 | tf_op jit(solution)/shard_map/all_gather | solution.py:102
  510.4 13.0 %convolution_convert_fusion = bf16[3072,512]{1,0:T(8,128)(2,1)} fusion(bf16[3072,2048]{1,0:T(8,128)(2,1)} %bitcast.49, bf16[2048,512]{1,0:T(8,128)(2,1)} %param.20), kind=kOutput, calls=%fused_computation.25 | convolution fusion | flops 6444023808 | bytes 17825792 | tf_op jit(solution)/shard_map/dot_general | solution.py:25
  523.3 5.5 reshape.253
  528.8 13.0 %convolution_convert_fusion.2 = bf16[3072,512]{1,0:T(8,128)(2,1)} fusion(bf16[3072,2048]{1,0:T(8,128)(2,1)} %bitcast.50, bf16[2048,512]{1,0:T(8,128)(2,1)} %param.21), kind=kOutput, calls=%fused_computation.27 | convolution fusion | flops 6444023808 | bytes 17825792 | tf_op jit(solution)/shard_map/dot_general | solution.py:28
  541.8 5.5 reshape.249
  547.3 5.1 fusion.8
  552.5 4.4 fusion.27
  556.9 3.1 select_convert_fusion
  560.0 4.6 copy.63
  (46 shorter events, 0.8 us)
Async XLA Ops:
  6.5 18.1 %copy-start = (bf16[16,128,512]{2,1,0:T(8,128)(2,1)S(1)}, bf16[16,128,512]{2,1,0:T(8,128)(2,1)}, u32[]{:S(2)}) copy-start(bf16[16,128,512]{2,1,0:T(8,128)(2,1)} %param.17) | copy-start | bytes 6291460
  8.8 1.0 copy-start.5
  8.8 2.4 copy-start.4
  13.9 23.5 %all-to-all-start = ((bf16[32,2,2]{1,2,0:T(2,128)(2,1)}), bf16[32,2,2]{1,2,0:T(2,128)(2,1)S(1)}, u32[]{:S(2)}, u32[]{:S(2)}) async-start(bf16[32,2,2]{1,2,0:T(2,128)(2,1)} %copy.47), calls=%async_computation | async-start | bytes 32768 | tf_op jit(solution)/shard_map/all_to_all | solution.py:94
  37.5 7.9 %copy-start.2 = (bf16[16,128,512]{2,1,0:T(8,128)(2,1)S(1)}, bf16[16,128,512]{2,1,0:T(8,128)(2,1)}, u32[]{:S(2)}) copy-start(bf16[16,128,512]{2,1,0:T(8,128)(2,1)} %param.18) | copy-start | bytes 6291460
  37.5 107.3 %all-to-all-start.1 = ((bf16[32,2,128,512]{3,2,1,0:T(8,128)(2,1)}), bf16[32,2,128,512]{3,2,1,0:T(8,128)(2,1)}, u32[]{:S(2)}, u32[]{:S(2)}) async-start(bf16[32,2,128,512]{3,2,1,0:T(8,128)(2,1)} %broadcast_select_fusion.1), calls=%async_computation.1 | async-start | bytes 16777216 | tf_op jit(solution)/shard_map/all_to_all | solution.py:92
  144.8 110.8 %all-to-all-start.2 = ((bf16[32,2,128,512]{3,2,1,0:T(8,128)(2,1)}), bf16[32,2,128,512]{3,2,1,0:T(8,128)(2,1)}, u32[]{:S(2)}, u32[]{:S(2)}) async-start(bf16[32,2,128,512]{3,2,1,0:T(8,128)(2,1)} %broadcast_select_fusion), calls=%async_computation.2 | async-start | bytes 16777216 | tf_op jit(solution)/shard_map/all_to_all | solution.py:93
  155.8 233.3 %all-gather.5.cloned.1.call-start = ((), (), s32[]{:S(2)}) async-start(), calls=%async_computation.4 | async-start | bytes 15728640 | tf_op jit(solution)/shard_map/all_gather | solution.py:103
  267.7 242.6 %all-gather.3.cloned.1.call-start = ((), (), s32[]{:S(2)}) async-start(), calls=%async_computation.3 | async-start | bytes 15728640 | tf_op jit(solution)/shard_map/all_gather | solution.py:102
  403.4 8.9 %copy-start.6 = (bf16[2048,512]{1,0:T(8,128)(2,1)S(1)}, bf16[2048,512]{1,0:T(8,128)(2,1)}, u32[]{:S(2)}) copy-start(bf16[2048,512]{1,0:T(8,128)(2,1)} %param.19) | copy-start | bytes 6291460
  552.5 4.4 copy-start.3
  556.9 7.8 %copy-start.1 = (bf16[16,128,512]{2,1,0:T(8,128)(2,1)S(1)}, bf16[16,128,512]{2,1,0:T(8,128)(2,1)}, u32[]{:S(2)}) copy-start(bf16[16,128,512]{2,1,0:T(8,128)(2,1)} %param.17) | copy-start | bytes 6291460
Sparse Core Ops, SparseCore 0:
  267.9 121.1 all-gather.4
  390.8 119.5 all-gather.2
where the time goes:
time: 573 us; the launch traced here: 572 us
  waiting for transfers between devices  384 us (67%)
  local copies, waits for them, and re-layouts  52.4 us (9%)
  other arithmetic  51.1 us (9%)
  matrix products  42.3 us (7%)
  starting transfers between devices  28.3 us (5%)
  between operations  13.7 us (2%)
    all_gather x1, waiting for transfers between devices, on_device(): lax.all_gather(rows_target, 'mp', axis=2, tiled=True)  119 us
    all_to_all x1, waiting for transfers between devices, on_device(): lax.all_to_all(send_target, 'dp', split_axis=0, concat_axis=0, tiled=True)  93.1 us
    all_to_all x1, waiting for transfers between devices, on_device(): lax.all_to_all(send_source, 'dp', split_axis=0, concat_axis=0, tiled=True)  86.6 us
    all_gather x1, waiting for transfers between devices, on_device(): lax.all_gather(rows_source, 'mp', axis=2, tiled=True)  84.3 us
    dot_general x1, matrix products, attend(): jnp.dot(source_rows.reshape(-1, D), w_value, preferred_element_type=jnp.f...  13 us
    dot_general x1, matrix products, attend(): jnp.dot(source_rows.reshape(-1, D), w_key, preferred_element_type=jnp.flo...  13 us
  transfers between devices with their start and end apart: 5, of which 4 were waited for; matrix products, arithmetic and copies ran while one was open for 13% of the time, Pallas kernels for 0%

commit v1 on v0

--- a/solution.py
+++ b/solution.py
@@ -99,7 +99,9 @@
     lengths_got = jnp.take(got_lengths.reshape(-1, 2), source, axis=0).astype(jnp.int32)
     lengths_got = jnp.where(usable[:, None], lengths_got, 0)
     full_source, full_target = (
-        lax.all_gather(rows_source, "mp", axis=2, tiled=True),
+        jnp.concatenate(
+            lax.all_to_all(jnp.stack([rows_source] * lax.axis_size("mp")), "mp", 0, 0), axis=2
+        ),
         lax.all_gather(rows_target, "mp", axis=2, tiled=True),
     )
     result = attend(

time: 573 us -> 624 us (1.089)
  waiting for transfers between devices: 384 us -> 410 us
  local copies, waits for them, and re-layouts: 52.4 us -> 66.7 us
  starting transfers between devices: 28.3 us -> 34.8 us
    all_to_all x0 -> x1, waiting for transfers between devices: none -> 232 us  [on_device(): lax.all_to_all(jnp.stack([rows_source] * lax.axis_size('mp')), 'mp', 0, 0)]
    all_gather x1, waiting for transfers between devices: 119 us -> 0.01 us  [on_device(): lax.all_gather(rows_target, 'mp', axis=2, tiled=True)]
    all_gather x1 -> x0, waiting for transfers between devices: 84.3 us -> none  [on_device(): lax.all_gather(rows_source, 'mp', axis=2, tiled=True)]
    another operation x0 -> x1, local copies, waits for them, and re-layouts: none -> 8.63 us  [on_device(): jnp.stack([rows_source] * lax.axis_size('mp'))]
    all_to_all x1, waiting for transfers between devices: 93.1 us -> 85.4 us  [on_device(): lax.all_to_all(send_target, 'dp', split_axis=0, concat_axis=0, tiled=True)]
    all_to_all x0 -> x1, starting transfers between devices: none -> 6.85 us  [on_device(): lax.all_to_all(jnp.stack([rows_source] * lax.axis_size('mp')), 'mp', 0, 0)]
    all_to_all x1, waiting for transfers between devices: 86.6 us -> 93.2 us  [on_device(): lax.all_to_all(send_source, 'dp', split_axis=0, concat_axis=0, tiled=True)]
  transfers between devices with their start and end apart: 5 -> 5, of which waited for: 4 -> 3; matrix products, arithmetic and copies ran while one was open for 13% -> 14% of each run, Pallas kernels for 0% -> 0%
where the time goes in v1:
time: 624 us; the launch traced here: 620 us
  waiting for transfers between devices  410 us (66%)
  local copies, waits for them, and re-layouts  66.7 us (11%)
  other arithmetic  50.5 us (8%)
  matrix products  44.5 us (7%)
  starting transfers between devices  34.8 us (6%)
  between operations  13.7 us (2%)
    all_to_all x1, waiting for transfers between devices, on_device(): lax.all_to_all(jnp.stack([rows_source] * lax.axis_size('mp')), 'mp', 0, 0)  232 us
    all_to_all x1, waiting for transfers between devices, on_device(): lax.all_to_all(send_source, 'dp', split_axis=0, concat_axis=0, tiled=True)  93.2 us
    all_to_all x1, waiting for transfers between devices, on_device(): lax.all_to_all(send_target, 'dp', split_axis=0, concat_axis=0, tiled=True)  85.4 us
    dot_general x1, matrix products, attend(): jnp.dot(source_rows.reshape(-1, D), w_value, preferred_element_type=jnp.f...  14.1 us
    dot_general x1, matrix products, attend(): jnp.dot(source_rows.reshape(-1, D), w_key, preferred_element_type=jnp.flo...  14.1 us
  transfers between devices with their start and end apart: 5, of which 3 were waited for; matrix products, arithmetic and copies ran while one was open for 14% of the time, Pallas kernels for 0%

profile of v1, /device:TPU:1, one launch (start us, length us, event | category | flops | bytes accessed | tf_op | source)
XLA Modules:
  0.0 620.3 jit_solution(15945683482600177351)
XLA Ops:
  6.5 0.9 compare_select_fusion.4
  7.4 0.8 slice_bitcast_fusion.2
  8.2 0.2 convert_reduce_fusion.1
  8.5 0.1 and_reduce_fusion
  8.5 0.1 fusion.29
  8.6 0.8 slice_bitcast_fusion.3
  9.4 0.1 copy.57
  9.5 0.1 reshape.364
  9.6 0.7 gather_fusion.3
  10.3 0.7 gather_fusion.1
  11.0 0.8 and_select_fusion.2
  11.7 0.8 gather_fusion.8
  12.5 0.8 gather_fusion.4
  13.3 0.8 gather_fusion.2
  14.1 0.1 reshape.367
  14.2 0.1 reshape.373
  14.4 0.1 reshape.387
  14.7 0.7 copy.61
  15.4 9.4 %all-to-all-start = ((bf16[32,2,2]{1,2,0:T(2,128)(2,1)}), bf16[32,2,2]{1,2,0:T(2,128)(2,1)S(1)}, u32[]{:S(2)}, u32[]{:S(2)}) async-start(bf16[32,2,2]{1,2,0:T(2,128)(2,1)} %copy.61), calls=%async_computation | async-start | bytes 32768 | tf_op jit(solution)/shard_map/all_to_all | solution.py:94
  24.8 0.1 copy.72
  24.9 0.1 copy.73
  25.0 0.1 reshape.388
  25.2 5.3 gather_fusion.9
  30.5 7.5 %broadcast_select_fusion = bf16[32,2,128,512]{3,2,1,0:T(8,128)(2,1)} fusion(bf16[32,2,128,512]{3,2,1,0:T(8,128)(2,1)} %bitcast.54, pred[32,2]{1,0:T(8,128)(4,1)S(1)} %copy.72), kind=kLoop, calls=%fused_computation.24 | loop fusion | flops 4194304 | bytes 16777280 | tf_op jit(solution)/shard_map/jit(_take)/select_n | solution.py:86
  38.0 7.4 %all-to-all-start.3 = ((bf16[32,2,128,512]{3,2,1,0:T(8,128)(2,1)}), bf16[32,2,128,512]{3,2,1,0:T(8,128)(2,1)}, u32[]{:S(2)}, u32[]{:S(2)}) async-start(bf16[32,2,128,512]{3,2,1,0:T(8,128)(2,1)} %broadcast_select_fusion), calls=%async_computation.3 | async-start | bytes 16777216 | tf_op jit(solution)/shard_map/all_to_all | solution.py:93
  45.4 0.8 gather_fusion.5
  46.2 0.1 reshape.377
  46.4 0.1 copy.67
  46.5 0.1 copy.68
  46.6 0.1 reshape.378
  46.7 0.3 copy-done.2
  47.0 5.3 gather_fusion.6
  52.3 7.5 %broadcast_select_fusion.1 = bf16[32,2,128,512]{3,2,1,0:T(8,128)(2,1)} fusion(bf16[32,2,128,512]{3,2,1,0:T(8,128)(2,1)} %bitcast.55, pred[32,2]{1,0:T(8,128)(4,1)S(1)} %copy.67), kind=kLoop, calls=%fused_computation.25 | loop fusion | flops 4194304 | bytes 16777280 | tf_op jit(solution)/shard_map/jit(_take)/select_n | solution.py:85
  59.8 85.4 %all-to-all-done.3 = bf16[32,2,128,512]{3,2,1,0:T(8,128)(2,1)} async-done(((bf16[32,2,128,512]{3,2,1,0:T(8,128)(2,1)}), bf16[32,2,128,512]{3,2,1,0:T(8,128)(2,1)}, u32[]{:S(2)}, u32[]{:S(2)}) %all-to-all-start.3) | async-done | bytes 8388640 | tf_op jit(solution)/shard_map/all_to_all | solution.py:93
  145.2 11.0 %all-to-all-start.1 = ((bf16[32,2,128,512]{3,2,1,0:T(8,128)(2,1)}), bf16[32,2,128,512]{3,2,1,0:T(8,128)(2,1)}, u32[]{:S(2)}, u32[]{:S(2)}) async-start(bf16[32,2,128,512]{3,2,1,0:T(8,128)(2,1)} %broadcast_select_fusion.1), calls=%async_computation.1 | async-start | bytes 16777216 | tf_op jit(solution)/shard_map/all_to_all | solution.py:92
  156.4 0.1 reduce-window.8
  156.5 0.1 reduce.1
  156.6 0.1 reshape.257
  156.7 0.1 select_reduce_fusion
  156.9 5.9 gather_fusion.10
  162.8 93.2 %all-to-all-done.1 = bf16[32,2,128,512]{3,2,1,0:T(8,128)(2,1)} async-done(((bf16[32,2,128,512]{3,2,1,0:T(8,128)(2,1)}), bf16[32,2,128,512]{3,2,1,0:T(8,128)(2,1)}, u32[]{:S(2)}, u32[]{:S(2)}) %all-to-all-start.1) | async-done | bytes 8388640 | tf_op jit(solution)/shard_map/all_to_all | solution.py:92
  255.9 5.9 gather_fusion.7
  261.8 6.2 broadcast_select_fusion.2
  268.0 4.9 copy.69
  272.9 8.6 %stack.19 = bf16[4,24,128,512]{2,1,3,0:T(8,128)(2,1)} broadcast(bf16[24,128,512]{1,0,2:T(8,128)(2,1)} %copy.69), dimensions={1,2,3} | broadcast | bytes 15728640 | tf_op jit(solution)/shard_map/stack | solution.py:103
  281.5 6.9 %all-to-all-start.2 = ((bf16[4,24,128,512]{2,1,3,0:T(8,128)(2,1)}), bf16[4,24,128,512]{2,1,3,0:T(8,128)(2,1)}, u32[]{:S(2)}, u32[]{:S(2)}) async-start(bf16[4,24,128,512]{2,1,3,0:T(8,128)(2,1)} %stack.19), calls=%async_computation.2 | async-start | bytes 25165824 | tf_op jit(solution)/shard_map/all_to_all | solution.py:103
  288.4 0.3 copy.80
  288.7 0.6 gather_fusion
  289.3 0.1 fusion.32
  289.5 0.2 fusion.30
  289.8 231.6 %all-to-all-done.2 = bf16[4,24,128,512]{2,1,3,0:T(8,128)(2,1)} async-done(((bf16[4,24,128,512]{2,1,3,0:T(8,128)(2,1)}), bf16[4,24,128,512]{2,1,3,0:T(8,128)(2,1)}, u32[]{:S(2)}, u32[]{:S(2)}) %all-to-all-start.2) | async-done | bytes 12582944 | tf_op jit(solution)/shard_map/all_to_all | solution.py:103
  521.4 14.1 %fusion.12 = bf16[3072,512]{1,0:T(8,128)(2,1)} fusion(bf16[2048,512]{1,0:T(8,128)(2,1)} %param.21, bf16[256,8,24,128]{3,2,1,0:T(8,128)(2,1)} %bitcast.22), kind=kOutput, calls=%fused_computation.31 | convolution fusion | flops 6444023808 | bytes 17825792 | tf_op jit(solution)/shard_map/dot_general | solution.py:28
  535.5 5.5 reshape.250
  541.0 14.1 %fusion.15 = bf16[3072,512]{1,0:T(8,128)(2,1)} fusion(bf16[2048,512]{1,0:T(8,128)(2,1)} %param.20, bf16[256,8,24,128]{3,2,1,0:T(8,128)(2,1)} %bitcast.22), kind=kOutput, calls=%fused_computation.32 | convolution fusion | flops 6444023808 | bytes 17825792 | tf_op jit(solution)/shard_map/dot_general | solution.py:25
  555.1 5.5 reshape.254
  560.6 6.3 %convert_reduce_fusion = f32[24,128]{1,0:T(8,128)S(1)} fusion(bf16[24,128,2048]{2,1,0:T(8,128)(2,1)} %all-gather.2.cloned.1.call-done), kind=kLoop, calls=%fused_computation.13 | loop fusion | flops 12579840 | bytes 12595200 | tf_op jit(solution)/shard_map/reduce_sum | solution.py:18
  566.9 8.0 %fusion.3 = f32[24,128]{1,0:T(8,128)S(1)} fusion(bf16[24,128,2048]{2,1,0:T(8,128)(2,1)} %all-gather.2.cloned.1.call-done, f32[24,128]{1,0:T(8,128)S(1)} %broadcast_multiply_fusion), kind=kLoop, calls=%fused_computation.16 | loop fusion | flops 25162752 | bytes 12607488 | tf_op jit(solution)/shard_map/reduce_sum | solution.py:20
  574.9 7.6 %fusion.4 = bf16[24,128,2048]{2,1,0:T(8,128)(2,1)S(1)} fusion(bf16[24,128,2048]{2,1,0:T(8,128)(2,1)} %all-gather.2.cloned.1.call-done, f32[24,128]{1,0:T(8,128)S(1)} %add_rsqrt_fusion, f32[24,128]{1,0:T(8,128)S(1)} %broadcast_multiply_fusion), kind=kLoop, calls=%fused_computation.17 | loop fusion | flops 25165824 | bytes 25190400 | tf_op jit(solution)/shard_map/convert_element_type | solution.py:21
  582.5 8.1 %convolution_convert_fusion = bf16[3072,512]{1,0:T(8,128)(2,1)} fusion(bf16[3072,2048]{1,0:T(8,128)(2,1)S(1)} %bitcast.56, bf16[2048,512]{1,0:T(8,128)(2,1)S(1)} %copy-done.4), kind=kOutput, calls=%fused_computation.33 | convolution fusion | flops 6444023808 | bytes 17825792 | tf_op jit(solution)/shard_map/dot_general | solution.py:22
  590.6 5.5 reshape.253
  596.2 5.1 fusion.20
  601.3 4.4 fusion.39
  605.7 3.1 select_convert_fusion
  608.9 4.6 copy.78
  (43 shorter events, 1.0 us)
Async XLA Ops:
  6.5 18.6 %copy-start = (bf16[16,128,512]{2,1,0:T(8,128)(2,1)S(1)}, bf16[16,128,512]{2,1,0:T(8,128)(2,1)}, u32[]{:S(2)}) copy-start(bf16[16,128,512]{2,1,0:T(8,128)(2,1)} %param.18) | copy-start | bytes 6291460
  15.4 22.6 %all-to-all-start = ((bf16[32,2,2]{1,2,0:T(2,128)(2,1)}), bf16[32,2,2]{1,2,0:T(2,128)(2,1)S(1)}, u32[]{:S(2)}, u32[]{:S(2)}) async-start(bf16[32,2,2]{1,2,0:T(2,128)(2,1)} %copy.61), calls=%async_computation | async-start | bytes 32768 | tf_op jit(solution)/shard_map/all_to_all | solution.py:94
  38.0 107.2 %all-to-all-start.3 = ((bf16[32,2,128,512]{3,2,1,0:T(8,128)(2,1)}), bf16[32,2,128,512]{3,2,1,0:T(8,128)(2,1)}, u32[]{:S(2)}, u32[]{:S(2)}) async-start(bf16[32,2,128,512]{3,2,1,0:T(8,128)(2,1)} %broadcast_select_fusion), calls=%async_computation.3 | async-start | bytes 16777216 | tf_op jit(solution)/shard_map/all_to_all | solution.py:93
  45.4 1.6 copy-start.2
  145.2 110.8 %all-to-all-start.1 = ((bf16[32,2,128,512]{3,2,1,0:T(8,128)(2,1)}), bf16[32,2,128,512]{3,2,1,0:T(8,128)(2,1)}, u32[]{:S(2)}, u32[]{:S(2)}) async-start(bf16[32,2,128,512]{3,2,1,0:T(8,128)(2,1)} %broadcast_select_fusion.1), calls=%async_computation.1 | async-start | bytes 16777216 | tf_op jit(solution)/shard_map/all_to_all | solution.py:92
  156.2 404.4 %all-gather.2.cloned.1.call-start = ((), (), s32[]{:S(2)}) async-start(), calls=%async_computation.4 | async-start | bytes 15728640 | tf_op jit(solution)/shard_map/all_gather | solution.py:105
  281.5 239.9 %all-to-all-start.2 = ((bf16[4,24,128,512]{2,1,3,0:T(8,128)(2,1)}), bf16[4,24,128,512]{2,1,3,0:T(8,128)(2,1)}, u32[]{:S(2)}, u32[]{:S(2)}) async-start(bf16[4,24,128,512]{2,1,3,0:T(8,128)(2,1)} %stack.19), calls=%async_computation.2 | async-start | bytes 25165824 | tf_op jit(solution)/shard_map/all_to_all | solution.py:103
  574.9 7.6 %copy-start.4 = (bf16[2048,512]{1,0:T(8,128)(2,1)S(1)}, bf16[2048,512]{1,0:T(8,128)(2,1)}, u32[]{:S(2)}) copy-start(bf16[2048,512]{1,0:T(8,128)(2,1)} %param.19) | copy-start | bytes 6291460
  601.3 4.4 copy-start.3
  605.7 7.8 %copy-start.1 = (bf16[16,128,512]{2,1,0:T(8,128)(2,1)S(1)}, bf16[16,128,512]{2,1,0:T(8,128)(2,1)}, u32[]{:S(2)}) copy-start(bf16[16,128,512]{2,1,0:T(8,128)(2,1)} %param.18) | copy-start | bytes 6291460
Sparse Core Ops, SparseCore 0:
  268.2 216.7 all-gather.1
